TPU v7x, 32 devices: a whole 2x2x4 slice. The times are simulated.
32 devices in a mesh: row: 4 (over y, x), col: 8 (over z, core).
Axes of the slice: x: 2, y: 2, z: 4, core: 2. Of those that a mesh axis runs over, the one named last changes fastest.
Arguments:
- coords: float32 [3, 4096], replicated, may hold values from 0 to 1
- lengths: float32 [3], replicated, may hold values from 0.4 to 1.2
- pattern: int32 [8, 8], replicated, may hold values from 0 to 1, as said below
- blocks: int32 [8], replicated, may hold values from 0 to 7, each once
- inverses: float32 [2, 512, 512], replicated, as said below
- earlier: bfloat16 [4096, 1024], P('row'), may hold values from -0.29882812 to 0.29882812
Outputs:
- schur: float32 [4096, 4096], P('row', 'col')
Inputs may be any that keep to these rules, and one draw needn't show every extreme that they name: `pattern`: symmetric, with ones on the diagonal. `blocks`: each tile gets its own site block. `inverses`: each of the two factors is lower triangular with a positive diagonal.
All inputs are finite; a program needn't handle non-finite values.
Results may differ from a plain program's by a relative error of at most 0.0007.
Values may be sent and summed in bfloat16 or wider, within the bound.
A program may use at most 64 MiB of HBM per device.

v0:
```python
import jax
import jax.numpy as jnp
from jax import lax
from jax.sharding import PartitionSpec as P

TB = 512


def from_root(block, axis, holder):
    block = jnp.where(lax.axis_index(axis) == holder, block, jnp.zeros_like(block))
    return lax.psum(block, axis)


def wendland(left_sites, right_sites):
    sq_dist = jnp.zeros((left_sites.shape[1], right_sites.shape[1]), jnp.float32)
    for component in range(3):
        offset = left_sites[component][:, None] - right_sites[component][None, :]
        sq_dist = sq_dist + offset * offset
    radius = jnp.sqrt(sq_dist)
    falloff = jnp.maximum(1.0 - radius, 0.0)
    return falloff**4 * (4.0 * radius + 1.0)


def outer_low(left_rows, right_rows):
    return lax.dot_general(
        left_rows, right_rows, (((1,), (1,)), ((), ())), preferred_element_type=jnp.float32
    )


def outer_high(left_rows, right_rows):
    return lax.dot_general(
        left_rows,
        right_rows,
        (((1,), (1,)), ((), ())),
        precision=lax.Precision.HIGHEST,
        preferred_element_type=jnp.float32,
    )


def tile_sites(coords, lengths, blocks, tile_ids):
    block_ids = jnp.take(blocks, tile_ids)
    picked = jnp.take(coords.reshape(3, -1, TB), block_ids, axis=1)
    return (picked / lengths[:, None, None]).reshape(3, -1)


def local(coords, lengths, pattern, blocks, inverses, earlier):
    row_count = lax.axis_size("row")
    col_count = lax.axis_size("col")
    row_index = lax.axis_index("row")
    col_index = lax.axis_index("col")
    tile_total = pattern.shape[0]
    row_tiles_n = tile_total // row_count
    col_tiles_n = tile_total // col_count
    row_tiles = jnp.arange(row_tiles_n, dtype=jnp.int32) * row_count + row_index
    col_tiles = jnp.arange(col_tiles_n, dtype=jnp.int32) * col_count + col_index
    row_sites = tile_sites(coords, lengths, blocks, row_tiles)
    col_sites = tile_sites(coords, lengths, blocks, col_tiles)
    panel_sites = tile_sites(coords, lengths, blocks, jnp.arange(2, dtype=jnp.int32))
    patf = pattern.astype(jnp.float32)
    row_pattern = jnp.take(patf, row_tiles, axis=0)
    panel_mask = jnp.repeat(row_pattern[:, :2], TB, axis=0)
    panel_earlier = []
    for panel_id in range(2):
        panel_earlier.append(from_root(earlier[:TB], "row", panel_id))
    column_earlier = []
    column_slot = 0
    tile_id = column_slot * col_count + col_index
    earlier_piece = lax.dynamic_slice_in_dim(earlier, tile_id // row_count * TB, TB, 0)
    column_earlier.append(from_root(earlier_piece, "row", tile_id % row_count))
    column_earlier = column_earlier[0]

    def panel_rows(sites, rows_earlier, mask, panel_id, previous, first_tile):
        cov = wendland(sites, panel_sites[:, panel_id * TB : (panel_id + 1) * TB]) * mask[:, None]
        cov = cov - outer_low(rows_earlier, panel_earlier[panel_id])
        if panel_id == 1:
            cov = cov - outer_high(previous, first_tile)
        return outer_high(cov, inverses[panel_id])

    first_panel = panel_rows(row_sites, earlier, panel_mask[:, 0], 0, None, None)
    tile_mask = jnp.zeros((TB,), jnp.float32) + patf[1, 0]
    first_tile = panel_rows(panel_sites[:, TB:], panel_earlier[1], tile_mask, 0, None, None)
    second_panel = panel_rows(row_sites, earlier, panel_mask[:, 1], 1, first_panel, first_tile)
    column_first = []
    column_second = []
    column_slot = 0
    tile_id = column_slot * col_count + col_index
    local_start = tile_id // row_count * TB
    first_piece = lax.dynamic_slice_in_dim(first_panel, local_start, TB, 0)
    second_piece = lax.dynamic_slice_in_dim(second_panel, local_start, TB, 0)
    got_first = from_root(first_piece.astype(jnp.bfloat16), "row", tile_id % row_count).astype(
        first_piece.dtype
    )
    got_second = from_root(second_piece.astype(jnp.bfloat16), "row", tile_id % row_count).astype(
        second_piece.dtype
    )
    column_first.append(got_first)
    column_second.append(got_second)
    column_first = column_first[0]
    column_second = column_second[0]
    block_mask = jnp.take(row_pattern, col_tiles, axis=1)
    cov = (
        wendland(row_sites, col_sites).reshape(row_tiles_n, TB, col_tiles_n, TB)
        * block_mask[:, None, :, None]
    )
    cov = cov.reshape(row_tiles_n * TB, col_tiles_n * TB)
    return (
        cov
        - outer_low(earlier, column_earlier)
        - outer_high(first_panel, column_first)
        - outer_high(second_panel, column_second)
    )


def solution(mesh):
    return jax.shard_map(
        local,
        mesh=mesh,
        in_specs=(P(), P(), P(), P(), P(), P("row", None)),
        out_specs=P("row", "col"),
        check_vma=False,
    )
```

profile of v0, /device:TPU:6, one launch (start us, length us, event | category | flops | bytes accessed | tf_op | source)
XLA Modules:
  0.0 198.7 jit_solution(8689045123374317837)
XLA Ops:
  6.5 3.7 %dynamic-slice_select_fusion = (bf16[512,1024]{1,0:T(8,128)(2,1)}, bf16[512,1024]{1,0:T(8,128)(2,1)}, bf16[512,1024]{1,0:T(8,128)(2,1)}) fusion(bf16[1024,1024]{1,0:T(8,128)(2,1)} %param.15, s32[]{:T(128)S(6)} %select_n.137, pred[]{:T(512)S(6)} %eq.15, pred[]{:T(512)S(6)} %eq.17, pred[]{:T(512)S(6)} %eq.16), kind=kLoop, calls=%fused_computation.63 | loop fusion | flops 1572864 | bytes 5242887 | tf_op jit(solution)/shard_map/jit(_where)/select_n | solution.py:10
  10.4 0.5 copy-done
  10.9 0.6 gather_fusion.1
  11.6 0.6 gather_fusion.3
  12.3 0.6 gather_fusion.2
  12.8 0.6 gather_fusion.4
  13.4 0.6 slice.104
  14.0 0.6 gather_fusion
  14.6 0.1 broadcast_select_fusion.2
  14.7 0.1 copy.10
  14.8 0.1 broadcast_bitcast_fusion
  14.9 0.1 bitcast_divide_fusion.1
  15.0 65.6 %all-reduce.7.cloned.1.call-done = (bf16[512,1024]{1,0:T(8,128)(2,1)}, bf16[512,1024]{1,0:T(8,128)(2,1)}) async-done(((bf16[512,1024]{1,0:T(8,128)(2,1)}, bf16[512,1024]{1,0:T(8,128)(2,1)}), (bf16[512,1024]{1,0:T(8,128)(2,1)}, bf16[512,1024]{1,0:T(8,128)(2,1)})) %all-reduce.7.cloned.1.call-update) | async-done | bytes 2097168 | tf_op jit(solution)/shard_map/psum | solution.py:11
  80.6 2.6 %fusion.82 = f32[512,1024]{1,0:T(8,128)S(1)} fusion(bf16[512,1024]{1,0:T(8,128)(2,1)} %get-tuple-element.43, bf16[1024,1024]{1,0:T(8,128)(2,1)S(1)} %copy-done.3), kind=kOutput, calls=%fused_computation.115 | convolution fusion | flops 1073741824 | bytes 5242880 | tf_op jit(solution)/shard_map/dot_general | solution.py:25
  83.2 1.3 fusion.84
  84.6 2.1 %convolution_subtract_fusion = f32[512,512]{1,0:T(8,128)S(1)} fusion(bf16[512,1024]{1,0:T(8,128)(2,1)S(1)} %copy-done.11, bf16[512,1024]{1,0:T(8,128)(2,1)S(1)} %copy-done.10, f32[]{:T(128)} %bitcast.28, f32[512]{0:T(512)S(1)} %bitcast.98, f32[512]{0:T(512)S(1)} %bitcast.94, f32[512]{0:T(512)S(1)} %bitcast.100, f32[512]{0:T(512)S(1)} %bitcast.96, ...), kind=kOutput, calls=%fused_computation.47 | convolution fusion | flops 541327360 | bytes 3158020 | tf_op jit(solution)/shard_map/dot_general | solution.py:25
  86.7 1.9 fusion.41
  88.6 8.3 %fusion.3 = f32[1024,512]{1,0:T(8,128)S(1)} fusion(f32[512,1024]{1,0:T(8,128)S(1)} %fusion.82, f32[1024]{0:T(1024)S(1)} %bitcast.91, f32[512]{0:T(512)S(1)} %bitcast.99, f32[512]{0:T(512)S(1)} %bitcast.101, f32[512]{0:T(512)S(1)} %bitcast.103, f32[1024]{0:T(1024)S(1)} %bitcast.84, f32[1024]{0:T(1024)S(1)} %bitcast.87, f32[1024]{0:T(1024)S(1)} %bitcast.81, ...), kind=kOutput, calls=%fused_computation.9 | convolution fusion | flops 3230138368 | bytes 5265408 | tf_op jit(solution)/shard_map/dot_general | solution.py:31
  96.9 0.9 fusion.67
  97.8 3.6 %fusion.85 = f32[1024,512]{0,1:T(8,128)S(1)} fusion(f32[1024,512]{1,0:T(8,128)S(1)} %fusion.3, f32[512,512]{1,0:T(8,128)S(1)} %fusion.41), kind=kOutput, calls=%fused_computation.118 | convolution fusion | flops 3221225472 | bytes 5242880 | tf_op jit(solution)/shard_map/dot_general | solution.py:31
  101.4 8.4 %fusion.1 = f32[1024,512]{1,0:T(8,128)S(1)} fusion(f32[1024,512]{0,1:T(8,128)S(1)} %fusion.85, f32[512,1024]{1,0:T(8,128)S(1)} %fusion.84, f32[2,512,512]{2,1,0:T(8,128)S(1)} %copy-done.5, f32[1024]{0:T(1024)S(1)} %bitcast.90, f32[512]{0:T(512)S(1)} %bitcast.95, f32[512]{0:T(512)S(1)} %bitcast.97, f32[512]{0:T(512)S(1)} %bitcast.93, f32[1024]{0:T(1024)S(1)} %bitcast.85, ...), kind=kOutput, calls=%fused_computation.7 | convolution fusion | flops 3230662656 | bytes 7362560 | tf_op jit(solution)/shard_map/dot_general | solution.py:31
  109.8 1.3 copy-done.1
  111.2 0.9 fusion.68
  112.1 0.6 dynamic-slice.8
  113.3 0.2 fusion.70
  113.4 0.1 broadcast_bitcast_fusion.1
  113.5 0.1 select_divide_fusion
  113.6 68.7 %all-reduce.5.cloned.1.call-done = (bf16[512,512]{1,0:T(8,128)(2,1)}, bf16[512,512]{1,0:T(8,128)(2,1)}, bf16[512,1024]{1,0:T(8,128)(2,1)}) async-done(((bf16[512,512]{1,0:T(8,128)(2,1)}, bf16[512,512]{1,0:T(8,128)(2,1)}, bf16[512,1024]{1,0:T(8,128)(2,1)}), (bf16[512,512]{1,0:T(8,128)(2,1)}, bf16[512,512]{1,0:T(8,128)(2,1)}, bf16[512,1024]{1,0:T(8,128)(2,1)})) %all-reduce.5.cloned.1.call-update) | async-done | bytes 2097168 | tf_op jit(solution)/shard_map/psum | solution.py:11
  182.3 3.1 %fusion.83 = f32[1024,512]{0,1:T(8,128)S(1)} fusion(f32[1024,512]{1,0:T(8,128)S(1)} %fusion.3, bf16[512,512]{1,0:T(8,128)(2,1)} %get-tuple-element.41), kind=kOutput, calls=%fused_computation.116 | convolution fusion | flops 3221225472 | bytes 4718592 | tf_op jit(solution)/shard_map/dot_general | solution.py:31
  185.5 1.9 fusion.86
  187.4 2.6 %fusion.5 = f32[1024,512]{0,1:T(8,128)S(1)} fusion(f32[1024,512]{0,1:T(8,128)S(1)} %fusion.86, f32[1024,512]{0,1:T(8,128)S(1)} %fusion.83, bf16[512,1024]{1,0:T(8,128)(2,1)S(1)} %copy-done.12, bf16[1024,1024]{1,0:T(8,128)(2,1)S(1)} %copy-done.4, f32[1024]{0:T(1024)S(1)} %bitcast.80, f32[512]{0:T(512)S(1)} %bitcast.105, f32[1024]{0:T(1024)S(1)} %bitcast.86, ...), kind=kOutput, calls=%fused_computation.12 | convolution fusion | flops 1083703296 | bytes 9459712 | tf_op jit(solution)/shard_map/dot_general | solution.py:25
  190.0 1.8 copy.13
  (45 shorter events, 0.3 us)
Async XLA Ops:
  6.5 74.0 %all-reduce.7.cloned.1.call-start = ((), (), s32[]{:S(2)}) async-start(), calls=%async_computation.1 | async-start | bytes 4194304 | tf_op jit(solution)/shard_map/psum | solution.py:11
  10.3 0.7 copy-start
  10.3 2.0 copy-start.7
  10.3 3.1 %copy-start.8 = (s32[8,8]{1,0:T(8,128)S(1)}, s32[8,8]{1,0:T(8,128)}, u32[]{:S(2)}) copy-start(s32[8,8]{1,0:T(8,128)} %param.12) | copy-start | bytes 772
  10.3 4.6 %copy-start.9 = (f32[3]{0:T(128)S(1)}, f32[3]{0:T(128)}, u32[]{:S(2)}) copy-start(f32[3]{0:T(128)} %param.11) | copy-start | bytes 40
  10.3 70.3 %copy-start.3 = (bf16[1024,1024]{1,0:T(8,128)(2,1)S(1)}, bf16[1024,1024]{1,0:T(8,128)(2,1)}, u32[]{:S(2)}) copy-start(bf16[1024,1024]{1,0:T(8,128)(2,1)} %param.15) | copy-start | bytes 6291460
  10.3 172.0 %all-reduce.5.cloned.1.call-start = ((), (), s32[]{:S(2)}) async-start(), calls=%async_computation | async-start | bytes 4194304 | tf_op jit(solution)/shard_map/psum | solution.py:11
  80.6 2.6 %copy-start.11 = (bf16[512,1024]{1,0:T(8,128)(2,1)S(1)}, bf16[512,1024]{1,0:T(8,128)(2,1)}, u32[]{:S(2)}) copy-start(bf16[512,1024]{1,0:T(8,128)(2,1)} %get-tuple-element.44) | copy-start | bytes 3145732
  83.2 1.3 copy-start.10
  84.5 2.1 %copy-start.5 = (f32[2,512,512]{2,1,0:T(8,128)S(1)}, f32[2,512,512]{2,1,0:T(8,128)}, u32[]{:S(2)}) copy-start(f32[2,512,512]{2,1,0:T(8,128)} %param.14) | copy-start | bytes 6291460
  109.8 1.3 copy-start.1
  182.3 3.1 %copy-start.2 = (f32[1024,512]{1,0:T(8,128)S(1)}, f32[1024,512]{1,0:T(8,128)}, u32[]{:S(2)}) copy-start(f32[1024,512]{1,0:T(8,128)} %copy-done.1) | copy-start | bytes 6291460
  182.3 3.1 %copy-start.6 = (bf16[512,512]{1,0:T(8,128)(2,1)S(1)}, bf16[512,512]{1,0:T(8,128)(2,1)}, u32[]{:S(2)}) copy-start(bf16[512,512]{1,0:T(8,128)(2,1)} %get-tuple-element.40) | copy-start | bytes 1572868
  185.4 2.0 copy-start.4
  185.4 2.0 copy-start.12
Sparse Core Ops, SparseCore 0:
  10.5 70.0 all-reduce.6
  112.2 70.0 all-reduce.4
where the time goes:
time: 201 us; the launch traced here: 199 us
  waiting for transfers between devices  134 us (67%)
  matrix products  35.8 us (18%)
  between operations  14.3 us (7%)
  local copies, waits for them, and re-layouts  8.13 us (4%)
  other arithmetic  6.06 us (3%)
    psum x2, waiting for transfers between devices, from_root(): return lax.psum(block, axis)  134 us
    dot_general x6, matrix products, outer_high(): lax.dot_general(left_rows, right_rows, (((1,), (1,)), ((), ())), precisio...  27.2 us
    dot_general x4, matrix products, outer_low(): lax.dot_general(left_rows, right_rows, (((1,), (1,)), ((), ())), preferre...  8.61 us
    select_n x3, other arithmetic, from_root(): jnp.where(lax.axis_index(axis) == holder, block, jnp.zeros_like(block))  5.57 us
  transfers between devices with their start and end apart: 2, of which 2 were waited for; matrix products, arithmetic and copies ran while one was open for 2% of the time, Pallas kernels for 0%

commit v1 on v0

v1 whole, which is shorter than its diff:
```python
import functools

import jax
import jax.numpy as jnp
from jax import lax
from jax.experimental import pallas as pl
from jax.experimental.pallas import tpu as pltpu
from jax.sharding import PartitionSpec as P

MESH = pl.DeviceIdType.MESH
BF = jnp.bfloat16
F32 = jnp.float32
PANELS = 2
PANEL_CHUNKS = 4
COL_CHUNKS = 4
STRIP = 32


def nt_dot(left, right):
    return lax.dot_general(left, right, (((1,), (1,)), ((), ())), preferred_element_type=F32)


def split3(x, order):
    hi = x.astype(BF)
    lo = (x - hi.astype(F32)).astype(BF)
    return jnp.concatenate([hi, hi, lo] if order == 0 else [hi, lo, hi], axis=1)


def tile_list(n_row, row_tiles_n):
    r = lax.axis_index("row")
    c = lax.axis_index("col")
    own = [jnp.int32(t * n_row) + r for t in range(row_tiles_n)]
    return own + [c, jnp.int32(1), jnp.int32(0)]


def pick_sites(n_row, row_tiles_n, lengths, blocks, coords, sites):
    tb = sites.shape[2]
    for t, tile in enumerate(tile_list(n_row, row_tiles_n)):
        start = pl.multiple_of(blocks[tile] * tb, 128)
        for comp in range(3):
            sites[t, comp : comp + 1, :] = coords[comp : comp + 1, pl.ds(start, tb)] / lengths[comp]
        sites[t, 3:8, :] = jnp.zeros((5, tb), F32)


def kernel(
    n_row,
    n_col,
    pattern,
    sites,
    earlier,
    inverses,
    out,
    got,
    sites_t,
    cov,
    inv_f,
    inv_s,
    low0,
    low1,
    send_sem,
    recv_sem,
    pair_sem,
    copy_sem,
    inv_sem,
):
    tb = inverses.shape[1]
    row_tiles_n = earlier.shape[0] // tb
    r = lax.axis_index("row")
    c = lax.axis_index("col")
    half = lax.rem(c, 2)
    mate = c + 1 - 2 * half
    bits = []
    b = n_row // 2
    while b:
        bits.append(b)
        b //= 2

    def flip(b):
        on = lax.rem(lax.div(r, b), 2)
        return r + b - 2 * b * on

    def distance(root):
        total = 0
        for b in bits:
            a1 = lax.rem(lax.div(r, b), 2)
            a2 = lax.rem(lax.div(root, b), 2)
            total = total + b * lax.rem(a1 + a2, 2)
        return total

    col_root = lax.rem(c, n_row)
    col_slot = lax.div(c, n_row)
    roots = [jnp.int32(p) for p in range(PANELS)] + [col_root]
    slots = [jnp.int32(0)] * PANELS + [col_slot]
    dist = [distance(root) for root in roots]

    half_rows = tb // 2
    p_rows = half_rows // PANEL_CHUNKS
    c_rows = tb // COL_CHUNKS
    streams = []
    for k in range(PANEL_CHUNKS):
        for p in range(PANELS):
            streams.append((p, half * half_rows + k * p_rows, p_rows, True))
    for k in range(COL_CHUNKS):
        streams.append((PANELS, jnp.int32(k * c_rows), c_rows, False))

    def piece(s, from_own):
        buf, first, rows, _ = streams[s]
        if from_own:
            start = pl.multiple_of(slots[buf] * tb + first, 16)
            return earlier.at[pl.ds(start, rows)]
        return got.at[buf, pl.ds(pl.multiple_of(first, 16), rows)]

    def row_copy(s, n, from_own):
        return pltpu.make_async_remote_copy(
            src_ref=piece(s, from_own),
            dst_ref=piece(s, False),
            send_sem=send_sem.at[s, n],
            recv_sem=recv_sem.at[s],
            device_id=(flip(bits[n]), c),
            device_id_type=MESH,
        )

    def pair_copy(s):
        return pltpu.make_async_remote_copy(
            src_ref=piece(s, False),
            dst_ref=piece(s, False),
            send_sem=send_sem.at[s, len(bits)],
            recv_sem=pair_sem.at[s],
            device_id=(r, mate),
            device_id_type=MESH,
        )

    def pair_arrival(s):
        buf, _, rows, _ = streams[s]
        k = s // PANELS
        first = pl.multiple_of((1 - half) * half_rows + k * p_rows, 16)
        there = got.at[buf, pl.ds(first, rows)]
        return pltpu.make_async_remote_copy(
            src_ref=there,
            dst_ref=there,
            send_sem=send_sem.at[s, len(bits)],
            recv_sem=pair_sem.at[s],
            device_id=(r, mate),
            device_id_type=MESH,
        )

    def sends(s, n):
        return lax.rem(dist[streams[s][0]], 2 * bits[n]) == 0

    def own_copy(buf):
        start = pl.multiple_of(slots[buf] * tb, 16)
        return pltpu.make_async_copy(
            earlier.at[pl.ds(start, tb)], got.at[buf], copy_sem.at[buf]
        )

    inv_copy = pltpu.make_async_copy(inverses, inv_f, inv_sem)
    inv_copy.start()

    barrier = pltpu.get_barrier_semaphore()
    for b in bits:
        pl.semaphore_signal(barrier, inc=1, device_id=(flip(b), c), device_id_type=MESH)
    pl.semaphore_signal(barrier, inc=1, device_id=(r, mate), device_id_type=MESH)
    pl.semaphore_wait(barrier, len(bits) + 1)

    for s in range(len(streams)):
        @pl.when(dist[streams[s][0]] == 0)
        def _(s=s):
            for n in range(len(bits)):
                row_copy(s, n, True).start()

    for buf in range(PANELS + 1):
        @pl.when(dist[buf] == 0)
        def _(buf=buf):
            own_copy(buf).start()

    def relay(s):
        @pl.when(dist[streams[s][0]] != 0)
        def _():
            row_copy(s, 0, False).wait_recv()
            for n in range(len(bits)):
                @pl.when(sends(s, n))
                def _(n=n):
                    row_copy(s, n, False).start()
            if streams[s][3]:
                pair_copy(s).start()

    def arrived(buf):
        @pl.when(dist[buf] == 0)
        def _():
            own_copy(buf).wait()

        for s in range(len(streams)):
            if streams[s][0] == buf and streams[s][3]:
                @pl.when(dist[buf] != 0)
                def _(s=s):
                    pair_arrival(s).wait_recv()

    tiles = tile_list(n_row, row_tiles_n)
    n_left = row_tiles_n + 2
    at_col, at_one, at_zero = row_tiles_n, row_tiles_n + 1, row_tiles_n + 2
    for t in range(n_left):
        sites_t[t] = sites[t].T

    def wendland(slot, left, right):
        keep = pattern[tiles[left], tiles[right]].astype(F32)

        def strip(i, carry):
            rows = pl.ds(pl.multiple_of(i * STRIP, STRIP), STRIP)
            at = sites_t[left, rows, :]
            sq = None
            for comp in range(3):
                off = at[:, comp : comp + 1] - sites[right, comp : comp + 1, :]
                sq = off * off if sq is None else sq + off * off
            radius = jnp.sqrt(sq)
            fall = jnp.maximum(1.0 - radius, 0.0)
            fall = fall * fall
            cov[slot, rows, :] = fall * fall * (4.0 * radius + 1.0) * keep
            return carry

        lax.fori_loop(0, tb // STRIP, strip, 0)

    def slot0(t):
        return t

    def slot1(t):
        return n_left + t

    def slot_out(t):
        return n_left + row_tiles_n + 1 + t

    covs = [(slot0(t), t, at_zero) for t in range(n_left)]
    covs += [(slot1(t), t, at_one) for t in range(row_tiles_n + 1)]
    covs += [(slot_out(t), t, at_col) for t in range(row_tiles_n)]
    n_panel = PANELS * PANEL_CHUNKS
    done = 0
    for n, (slot, left, right) in enumerate(covs):
        wendland(slot, left, right)
        if n >= 1 and done < n_panel:
            relay(done)
            done += 1
    while done < n_panel:
        relay(done)
        done += 1

    inv_copy.wait()
    for p in range(PANELS):
        inv_s[p] = split3(inv_f[p], 1)

    def own_rows(t):
        return earlier[pl.ds(t * tb, tb), :]

    def panel0(t, rows_u):
        p0 = cov[slot0(t)] - nt_dot(rows_u, got[0])
        low0[t] = nt_dot(split3(p0, 0), inv_s[0]).astype(BF)

    def panel1(t, rows_u):
        p1 = cov[slot1(t)] - nt_dot(rows_u, got[1]) - nt_dot(low0[t], low0[at_one])
        low1[t] = nt_dot(split3(p1, 0), inv_s[1]).astype(BF)

    arrived(0)
    for t in range(row_tiles_n):
        panel0(t, own_rows(t))
        if done < len(streams):
            relay(done)
            done += 1
    arrived(1)
    panel0(at_one, got[1])
    if done < len(streams):
        relay(done)
        done += 1
    for t in range(row_tiles_n):
        panel1(t, own_rows(t))
        if done < len(streams):
            relay(done)
            done += 1
    while done < len(streams):
        relay(done)
        done += 1
    arrived(PANELS)
    panel0(at_col, got[PANELS])
    panel1(at_col, got[PANELS])
    for t in range(row_tiles_n):
        out[pl.ds(t * tb, tb), :] = (
            cov[slot_out(t)]
            - nt_dot(own_rows(t), got[PANELS])
            - nt_dot(low0[t], low0[at_col])
            - nt_dot(low1[t], low1[at_col])
        )

    for s in range(len(streams)):
        for n in range(len(bits)):
            @pl.when(sends(s, n))
            def _(s=s, n=n):
                row_copy(s, n, False).wait_send()
        if streams[s][3]:
            @pl.when(dist[streams[s][0]] != 0)
            def _(s=s):
                pair_copy(s).wait_send()


def solution(mesh):
    n_row, n_col = mesh.shape["row"], mesh.shape["col"]
    n_bits = n_row.bit_length() - 1

    def local(coords, lengths, pattern, blocks, inverses, earlier):
        tb = inverses.shape[1]
        rows, width = earlier.shape
        row_tiles_n = rows // tb
        assert pattern.shape[0] == n_col and n_row == 1 << n_bits
        n_streams = PANELS * PANEL_CHUNKS + COL_CHUNKS
        n_left = row_tiles_n + 2
        smem = pl.BlockSpec(memory_space=pltpu.SMEM)
        vmem = pl.BlockSpec(memory_space=pltpu.VMEM)
        anym = pl.BlockSpec(memory_space=pl.ANY)
        sites = pl.pallas_call(
            functools.partial(pick_sites, n_row, row_tiles_n),
            out_shape=jax.ShapeDtypeStruct((n_left + 1, 8, tb), F32),
            in_specs=[smem, smem, vmem],
            out_specs=vmem,
        )(lengths, blocks, coords)
        return pl.pallas_call(
            functools.partial(kernel, n_row, n_col),
            out_shape=jax.ShapeDtypeStruct((rows, tb), F32),
            in_specs=[smem, vmem, vmem, anym],
            out_specs=vmem,
            scratch_shapes=[
                pltpu.VMEM((PANELS + 1, tb, width), BF),
                pltpu.VMEM((n_left, tb, 8), F32),
                pltpu.VMEM((n_left + 2 * row_tiles_n + 1, tb, tb), F32),
                pltpu.VMEM((PANELS, tb, tb), F32),
                pltpu.VMEM((PANELS, tb, 3 * tb), BF),
                pltpu.VMEM((n_left, tb, tb), BF),
                pltpu.VMEM((n_left, tb, tb), BF),
                pltpu.SemaphoreType.DMA((n_streams, n_bits + 1)),
                pltpu.SemaphoreType.DMA((n_streams,)),
                pltpu.SemaphoreType.DMA((n_streams,)),
                pltpu.SemaphoreType.DMA((PANELS + 1,)),
                pltpu.SemaphoreType.DMA,
            ],
            compiler_params=pltpu.CompilerParams(
                collective_id=0, has_side_effects=True, vmem_limit_bytes=56 * 1024 * 1024
            ),
        )(pattern, sites, earlier, inverses)

    return jax.shard_map(
        local,
        mesh=mesh,
        in_specs=(P(), P(), P(), P(), P(), P("row", None)),
        out_specs=P("row", "col"),
        check_vma=False,
    )
```

time: 201 us -> 85 us (0.42)
  waiting for transfers between devices: 134 us -> 0 us
  Pallas kernels: 0 us -> 80.6 us
  matrix products: 35.8 us -> 0 us
  between operations: 14.3 us -> 0.01 us
  other arithmetic: 6.06 us -> 0 us
  local copies, waits for them, and re-layouts: 8.13 us -> 3.08 us
    psum x2 -> x0, waiting for transfers between devices: 134 us -> none  [from_root(): return lax.psum(block, axis)]
    pallas_call x0 -> x2, Pallas kernels: none -> 80.6 us  [the longest x1 79.1 us: local(): pl.pallas_call(functools.partial(kernel, n_row, n_col), out_shape=jax.Sha...]
    dot_general x10 -> x0, matrix products: 35.8 us -> none  [the longest x6 27.2 us: outer_high(): lax.dot_general(left_rows, right_rows, (((1,), (1,)), ((), ())), precisio...]
    select_n x7 -> x0, other arithmetic: 5.85 us -> none  [the longest x3 5.57 us: from_root(): jnp.where(lax.axis_index(axis) == holder, block, jnp.zeros_like(block))]
    gather x6 -> x0, local copies, waits for them, and re-layouts: 3.56 us -> none  [the longest x3 1.86 us: tile_sites(): block_ids = jnp.take(blocks, tile_ids)]
  transfers between devices with their start and end apart: 2 -> 0, of which waited for: 2 -> 0; matrix products, arithmetic and copies ran while one was open for 2% -> 0% of each run, Pallas kernels for 0% -> 0%
where the time goes in v1:
time: 85 us; the launch traced here: 83.7 us
  Pallas kernels  80.6 us (95%)
  local copies, waits for them, and re-layouts  3.08 us (4%)
    pallas_call x1, Pallas kernels, local(): pl.pallas_call(functools.partial(kernel, n_row, n_col), out_shape=jax.Sha...  79.1 us
    unnamed x1, local copies, waits for them, and re-layouts  3.08 us

profile of v1, /device:TPU:6, one launch (start us, length us, event | category | flops | bytes accessed | tf_op | source)
XLA Modules:
  0.0 83.7 jit_solution(6946884747543055014)
XLA Ops:
  0.0 1.5 %shard_map.64.sites = f32[5,8,512]{2,1,0:T(8,128)} custom-call(f32[3]{0:T(128)} %lengths.1, s32[8]{0:T(128)} %blocks.1, f32[3,4096]{1,0:T(4,128)} %coords.1), custom_call_target="tpu_custom_call" | custom-call | tf_op jit(solution)/shard_map/pallas_call | solution.py:315
  1.5 79.1 %shard_map.65 = f32[1024,512]{1,0:T(8,128)} custom-call(s32[8,8]{1,0:T(8,128)} %pattern.1, f32[5,8,512]{2,1,0:T(8,128)} %shard_map.64.sites, bf16[1024,1024]{1,0:T(8,128)(2,1)} %earlier.1, f32[2,512,512]{2,1,0:T(8,128)} %inverses.1), custom_call_target="tpu_custom_call" | custom-call | tf_op jit(solution)/shard_map/pallas_call | solution.py:321
  80.6 3.1 %copy.8 = f32[1024,512]{1,0:T(8,128)} copy(f32[1024,512]{1,0:T(8,128)} %shard_map.65) | data formatting | bytes 4194304

commit v2 on v1

--- a/solution.py
+++ b/solution.py
@@ -162,11 +162,16 @@
     pl.semaphore_signal(barrier, inc=1, device_id=(r, mate), device_id_type=MESH)
     pl.semaphore_wait(barrier, len(bits) + 1)
 
-    for s in range(len(streams)):
+    n_panel = PANELS * PANEL_CHUNKS
+
+    def launch(s):
         @pl.when(dist[streams[s][0]] == 0)
-        def _(s=s):
+        def _():
             for n in range(len(bits)):
                 row_copy(s, n, True).start()
+
+    for s in range(n_panel):
+        launch(s)
 
     for buf in range(PANELS + 1):
         @pl.when(dist[buf] == 0)
@@ -231,20 +236,26 @@
     covs = [(slot0(t), t, at_zero) for t in range(n_left)]
     covs += [(slot1(t), t, at_one) for t in range(row_tiles_n + 1)]
     covs += [(slot_out(t), t, at_col) for t in range(row_tiles_n)]
-    n_panel = PANELS * PANEL_CHUNKS
     done = 0
+    sent = n_panel
     for n, (slot, left, right) in enumerate(covs):
         wendland(slot, left, right)
+        if n == 1:
+            inv_copy.wait()
+            for p in range(PANELS):
+                inv_s[p] = split3(inv_f[p], 1)
         if n >= 1 and done < n_panel:
             relay(done)
             done += 1
+            if done >= n_panel // 2 and sent < len(streams):
+                launch(sent)
+                sent += 1
     while done < n_panel:
         relay(done)
         done += 1
-
-    inv_copy.wait()
-    for p in range(PANELS):
-        inv_s[p] = split3(inv_f[p], 1)
+    while sent < len(streams):
+        launch(sent)
+        sent += 1
 
     def own_rows(t):
         return earlier[pl.ds(t * tb, tb), :]
@@ -260,7 +271,7 @@
     arrived(0)
     for t in range(row_tiles_n):
         panel0(t, own_rows(t))
-        if done < len(streams):
+        if t >= 1 and done < len(streams):
             relay(done)
             done += 1
     arrived(1)

time: 85 us -> 82 us (0.965); the launches traced: 83.7 us -> 81.8 us
  Pallas kernels: 80.6 us -> 78.7 us
    pallas_call x1, Pallas kernels: 79.1 us -> 77.2 us  [local(): pl.pallas_call(functools.partial(kernel, n_row, n_col), out_shape=jax.Sha...]
where the time goes in v2:
time: 82 us; the launch traced here: 81.8 us
  Pallas kernels  78.7 us (96%)
  local copies, waits for them, and re-layouts  3.08 us (4%)
    pallas_call x1, Pallas kernels, local(): pl.pallas_call(functools.partial(kernel, n_row, n_col), out_shape=jax.Sha...  77.2 us
    unnamed x1, local copies, waits for them, and re-layouts  3.08 us

profile of v2, /device:TPU:6, one launch (start us, length us, event | category | flops | bytes accessed | tf_op | source)
XLA Modules:
  0.0 81.8 jit_solution(5814969122562854961)
XLA Ops:
  0.0 1.5 %shard_map.64.sites = f32[5,8,512]{2,1,0:T(8,128)} custom-call(f32[3]{0:T(128)} %lengths.1, s32[8]{0:T(128)} %blocks.1, f32[3,4096]{1,0:T(4,128)} %coords.1), custom_call_target="tpu_custom_call" | custom-call | tf_op jit(solution)/shard_map/pallas_call | solution.py:326
  1.5 77.2 %shard_map.65 = f32[1024,512]{1,0:T(8,128)} custom-call(s32[8,8]{1,0:T(8,128)} %pattern.1, f32[5,8,512]{2,1,0:T(8,128)} %shard_map.64.sites, bf16[1024,1024]{1,0:T(8,128)(2,1)} %earlier.1, f32[2,512,512]{2,1,0:T(8,128)} %inverses.1), custom_call_target="tpu_custom_call" | custom-call | tf_op jit(solution)/shard_map/pallas_call | solution.py:332
  78.7 3.1 %copy.8 = f32[1024,512]{1,0:T(8,128)} copy(f32[1024,512]{1,0:T(8,128)} %shard_map.65) | data formatting | bytes 4194304
